TPU v7x, 128 devices: a whole 4x4x4 slice. The times are simulated.
128 devices in a mesh: grp: 8 (over z, core), ep: 16 (over x, y).
Axes of the slice: x: 4, y: 4, z: 4, core: 2. Of those that a mesh axis runs over, the one named last changes fastest.
Arguments:
- tokens: bfloat16 [4096, 7168], P('ep'), may hold values from -6 to 6
- cotangent: bfloat16 [4096, 7168], P('ep'), may hold values from -6 to 6
- expert_ids: int32 [4096, 8], P('ep'), may hold values from 0 to 255, as said below
- gate_scores: float32 [4096, 8], P('ep'), may hold values from 0.1 to 1
- gate_weight: bfloat16 [16, 7168, 1024], P('ep', None, 'grp'), may hold values from -0.0625 to 0.0625
- up_weight: bfloat16 [16, 7168, 1024], P('ep', None, 'grp'), may hold values from -0.0625 to 0.0625
- down_weight: bfloat16 [16, 1024, 7168], P('ep', 'grp'), may hold values from -0.1875 to 0.1875
Outputs:
- grad_tokens: bfloat16 [4096, 7168], P('ep')
- grad_gate_weight: bfloat16 [16, 7168, 1024], P('ep', None, 'grp')
- grad_up_weight: bfloat16 [16, 7168, 1024], P('ep', None, 'grp')
- grad_down_weight: bfloat16 [16, 1024, 7168], P('ep', 'grp')
Inputs may be any that keep to these rules, and one draw needn't show every extreme that they name: `expert_ids`: the 8 numbers of a row differ; a row names at most one number below 16; among the 256 rows of one index of ep (aligned blocks), at most 24 name the same number below 16.
All inputs are finite; a program needn't handle non-finite values.
Results may differ from a plain program's by a relative error of at most 0.0057.
Values may be sent and summed in bfloat16 or wider, within the bound.
A program may use at most 128 MiB of HBM per device.

v0:
```python
import jax
import jax.numpy as jnp
from jax import lax
from jax.sharding import PartitionSpec as P

MOST = 24


def block_slots(block_ids, block_gates, window, bound):
    row_count = block_ids.shape[0]
    flat_ids = block_ids.reshape(-1)
    occupied = flat_ids < window
    onehot = (flat_ids[:, None] == jnp.arange(window, dtype=jnp.int32)[None, :]).astype(jnp.int32)
    before = jnp.cumsum(onehot, axis=0) - onehot
    slot_rank = jnp.sum(before * onehot, axis=1)
    destination = jnp.where(occupied, flat_ids * bound + slot_rank, window * bound)
    pair_token = jnp.arange(flat_ids.shape[0], dtype=jnp.int32) // block_ids.shape[1]
    slot_token = (
        jnp.full((window * bound + 1,), row_count, jnp.int32)
        .at[destination]
        .set(pair_token)[: window * bound]
    )
    slot_gate = (
        jnp.zeros((window * bound + 1,), jnp.float32)
        .at[destination]
        .set(block_gates.reshape(-1))[: window * bound]
    )
    return (slot_token, slot_gate)


def backward_rows(rows_x, rows_c, gate_w, up_w, down_w):
    gate_pre = jnp.dot(rows_x, gate_w, preferred_element_type=jnp.float32)
    up_pre = jnp.dot(rows_x, up_w, preferred_element_type=jnp.float32)
    sigmoid_gate = jax.nn.sigmoid(gate_pre)
    activated = gate_pre * sigmoid_gate
    hidden = (activated * up_pre).astype(jnp.bfloat16)
    grad_hidden = jnp.dot(rows_c, down_w.T, preferred_element_type=jnp.float32)
    grad_up = (grad_hidden * activated).astype(jnp.bfloat16)
    grad_gate = (
        grad_hidden * up_pre * sigmoid_gate * (1.0 + gate_pre * (1.0 - sigmoid_gate))
    ).astype(jnp.bfloat16)
    down_grad = jnp.dot(hidden.T, rows_c, preferred_element_type=jnp.float32)
    gate_grad = jnp.dot(rows_x.T, grad_gate, preferred_element_type=jnp.float32)
    up_grad = jnp.dot(rows_x.T, grad_up, preferred_element_type=jnp.float32)
    row_grad = jnp.dot(grad_gate, gate_w.T, preferred_element_type=jnp.float32) + jnp.dot(
        grad_up, up_w.T, preferred_element_type=jnp.float32
    )
    return (gate_grad, up_grad, down_grad, row_grad)


def combine_rows(back_rows, slot_token, row_count):
    flat_rows = back_rows.reshape(-1, back_rows.shape[-1]).astype(jnp.float32)
    summed = (
        jnp.zeros((row_count + 1, flat_rows.shape[1]), jnp.float32).at[slot_token].add(flat_rows)
    )
    return summed[:row_count].astype(jnp.bfloat16)


def per_device(tokens, cotangent, expert_ids, gate_scores, gate_weight, up_weight, down_weight):
    groups = lax.axis_size("ep")
    row_count = tokens.shape[0]
    features = tokens.shape[1]
    slot_token, slot_gate = block_slots(expert_ids, gate_scores, groups, MOST)
    pad_tokens = jnp.concatenate([tokens, jnp.zeros((1, features), tokens.dtype)], axis=0)
    pad_cotangent = jnp.concatenate([cotangent, jnp.zeros((1, features), cotangent.dtype)], axis=0)
    send_x = pad_tokens[slot_token].reshape(groups, MOST, features)
    send_c = (
        (slot_gate[:, None] * pad_cotangent[slot_token].astype(jnp.float32))
        .astype(jnp.bfloat16)
        .reshape(groups, MOST, features)
    )
    recv_x, recv_c = (
        lax.all_to_all(send_x, "ep", split_axis=0, concat_axis=0, tiled=True),
        lax.all_to_all(send_c, "ep", split_axis=0, concat_axis=0, tiled=True),
    )
    rows_x = recv_x.reshape(-1, features)
    rows_c = recv_c.reshape(-1, features)
    gate_w = gate_weight[0]
    up_w = up_weight[0]
    down_w = down_weight[0]
    gate_grad, up_grad, down_grad, row_grad = backward_rows(rows_x, rows_c, gate_w, up_w, down_w)
    partial_rows = row_grad.reshape(groups, MOST, features)
    whole = lax.psum(partial_rows, "grp").astype(jnp.bfloat16)
    back_whole = lax.all_to_all(whole, "ep", split_axis=0, concat_axis=0, tiled=True)
    grad_tokens = combine_rows(back_whole, slot_token, row_count)
    return (
        grad_tokens,
        gate_grad.astype(jnp.bfloat16)[None],
        up_grad.astype(jnp.bfloat16)[None],
        down_grad.astype(jnp.bfloat16)[None],
    )


def solution(mesh):
    placed = (
        P("ep", None),
        P("ep", None),
        P("ep", None),
        P("ep", None),
        P("ep", None, "grp"),
        P("ep", None, "grp"),
        P("ep", "grp", None),
    )
    return jax.shard_map(
        per_device,
        mesh=mesh,
        in_specs=placed,
        out_specs=(P("ep", None), P("ep", None, "grp"), P("ep", None, "grp"), P("ep", "grp", None)),
        check_vma=False,
    )
```

profile of v0, /device:TPU:28, one launch (start us, length us, event | category | flops | bytes accessed | tf_op | source)
XLA Modules:
  0.0 461.5 jit_solution(8078474176963358665)
XLA Ops:
  3.8 4.5 reduce-window.6
  9.2 8.0 %scatter_custom_fusion = s32[385]{0:T(512)S(1)} fusion(s32[2048]{0:T(1024)S(1)} %bitcast.69, s32[2048]{0:T(1024)S(1)} %add_select_fusion, s32[]{:T(128)} %constant.13.clone.1), kind=kCustom, calls=%fused_computation.55 | custom fusion | bytes 1544 | tf_op jit(solution)/shard_map/scatter | solution.py:21
  17.2 4.4 concatenate.7
  21.6 15.8 %gather_fusion.1 = bf16[384,7168]{1,0:T(8,128)(2,1)} fusion(bf16[257,7168]{1,0:T(8,128)(2,1)} %concatenate.7, s32[1024]{0:T(1024)S(1)} %pad_clamp_fusion), kind=kCustom, calls=%fused_computation.1 | custom fusion | bytes 11011584 | tf_op jit(solution)/shard_map/gather | solution.py:66
  37.4 7.2 %all-to-all-start.1 = ((bf16[16,24,7168]{2,1,0:T(8,128)(2,1)}), bf16[16,24,7168]{2,1,0:T(8,128)(2,1)}, u32[]{:S(2)}, u32[]{:S(2)}) async-start(bf16[16,24,7168]{2,1,0:T(8,128)(2,1)} %bitcast.63), calls=%async_computation.1 | async-start | bytes 11010048 | tf_op jit(solution)/shard_map/all_to_all | solution.py:73
  44.9 8.3 %scatter_custom_fusion.1 = f32[385]{0:T(512)S(1)} fusion(s32[2048]{0:T(1024)S(1)} %bitcast.70, f32[2048]{0:T(1024)S(1)} %reshape.132, f32[]{:T(128)} %constant.14.clone.1), kind=kCustom, calls=%fused_computation.53 | custom fusion | bytes 1544 | tf_op jit(solution)/shard_map/scatter | solution.py:26
  53.3 4.4 concatenate.6
  57.6 15.8 %gather_fusion = bf16[384,7168]{1,0:T(8,128)(2,1)} fusion(bf16[257,7168]{1,0:T(8,128)(2,1)} %concatenate.6, s32[1024]{0:T(1024)S(1)} %pad_clamp_fusion), kind=kCustom, calls=%fused_computation | custom fusion | bytes 11011584 | tf_op jit(solution)/shard_map/gather | solution.py:68
  73.5 6.7 %fusion.2 = bf16[16,24,7168]{2,1,0:T(8,128)(2,1)} fusion(bf16[16,24,7168]{2,1,0:T(8,128)(2,1)} %bitcast.64, f32[16,24]{1,0:T(8,128)S(1)} %mul.55), kind=kLoop, calls=%fused_computation.8 | loop fusion | flops 8257536 | bytes 11011584 | tf_op jit(solution)/shard_map/convert_element_type | solution.py:69
  80.2 55.3 %all-to-all-done.1 = bf16[16,24,7168]{2,1,0:T(8,128)(2,1)} async-done(((bf16[16,24,7168]{2,1,0:T(8,128)(2,1)}), bf16[16,24,7168]{2,1,0:T(8,128)(2,1)}, u32[]{:S(2)}, u32[]{:S(2)}) %all-to-all-start.1) | async-done | bytes 5505056 | tf_op jit(solution)/shard_map/all_to_all | solution.py:73
  135.5 7.5 %all-to-all-start = ((bf16[16,24,7168]{2,1,0:T(8,128)(2,1)}), bf16[16,24,7168]{2,1,0:T(8,128)(2,1)}, u32[]{:S(2)}, u32[]{:S(2)}) async-start(bf16[16,24,7168]{2,1,0:T(8,128)(2,1)} %fusion.2), calls=%async_computation | async-start | bytes 11010048 | tf_op jit(solution)/shard_map/all_to_all | solution.py:74
  143.1 4.3 fusion.9
  147.4 4.2 fusion.12
  151.5 58.6 %all-to-all-done = bf16[16,24,7168]{2,1,0:T(8,128)(2,1)} async-done(((bf16[16,24,7168]{2,1,0:T(8,128)(2,1)}), bf16[16,24,7168]{2,1,0:T(8,128)(2,1)}, u32[]{:S(2)}, u32[]{:S(2)}) %all-to-all-start) | async-done | bytes 5505056 | tf_op jit(solution)/shard_map/all_to_all | solution.py:74
  210.2 4.7 %multiply_convert_fusion.1 = (bf16[384,128]{1,0:T(8,128)(2,1)S(1)}, bf16[384,128]{1,0:T(8,128)(2,1)S(1)}) fusion(f32[384,128]{1,0:T(8,128)S(1)} %fusion.9, f32[384,128]{1,0:T(8,128)S(1)} %fusion.12, bf16[384,7168]{1,0:T(8,128)(2,1)} %bitcast.4, bf16[1,128,7168]{2,1,0:T(8,128)(2,1)} %param.13), kind=kOutput, calls=%fused_computation.28 | convolution fusion | flops 705282048 | bytes 7929856 | tf_op jit(solution)/shard_map/dot_general | solution.py:37
  216.5 5.9 %convolution_add_fusion = f32[384,7168]{1,0:T(8,128)} fusion(f32[384,7168]{1,0:T(8,128)S(1)} %fusion.7, bf16[384,128]{1,0:T(8,128)(2,1)S(1)} %get-tuple-element.4, bf16[1,7168,128]{2,1,0:T(8,128)(2,1)S(1)} %copy-done.2), kind=kOutput, calls=%fused_computation.9 | convolution fusion | flops 707395584 | bytes 23953408 | tf_op jit(solution)/shard_map/dot_general | solution.py:45
  222.4 116.8 %all-reduce.3 = bf16[16,24,7168]{2,1,0:T(8,128)(2,1)} all-reduce(f32[16,24,7168]{2,1,0:T(8,128)} %bitcast.62), channel_id=1, replica_groups=mesh['grp'=8,'ep'=16] {'grp'}, use_global_device_ids=true, to_apply=%region_5.6 | all-reduce | flops 2752512 | bytes 16515072 | tf_op jit(solution)/shard_map/psum | solution.py:83
  339.1 6.9 %all-to-all-start.2 = ((bf16[16,24,7168]{2,1,0:T(8,128)(2,1)}), bf16[16,24,7168]{2,1,0:T(8,128)(2,1)}, u32[]{:S(2)}, u32[]{:S(2)}) async-start(bf16[16,24,7168]{2,1,0:T(8,128)(2,1)} %all-reduce.3), calls=%async_computation.2 | async-start | bytes 11010048 | tf_op jit(solution)/shard_map/all_to_all | solution.py:84
  346.1 5.4 %fusion.4 = bf16[1,7168,128]{2,1,0:T(8,128)(2,1)} fusion(bf16[384,7168]{1,0:T(8,128)(2,1)} %bitcast.7, bf16[384,128]{1,0:T(8,128)(2,1)S(1)} %get-tuple-element.4), kind=kOutput, calls=%fused_computation.14 | convolution fusion | flops 705560576 | bytes 7438336 | tf_op jit(solution)/shard_map/dot_general | solution.py:44
  351.5 5.4 %fusion.3 = bf16[1,7168,128]{2,1,0:T(8,128)(2,1)} fusion(bf16[384,7168]{1,0:T(8,128)(2,1)} %bitcast.7, bf16[384,128]{1,0:T(8,128)(2,1)S(1)} %get-tuple-element.5), kind=kOutput, calls=%fused_computation.13 | convolution fusion | flops 705560576 | bytes 7438336 | tf_op jit(solution)/shard_map/dot_general | solution.py:43
  356.9 5.0 %fusion.5 = bf16[1,128,7168]{2,1,0:T(8,128)(2,1)} fusion(bf16[384,7168]{1,0:T(8,128)(2,1)} %bitcast.4, f32[384,128]{1,0:T(8,128)S(1)} %fusion.12, f32[384,128]{1,0:T(8,128)S(1)} %fusion.9), kind=kOutput, calls=%fused_computation.15 | convolution fusion | flops 705855488 | bytes 7733248 | tf_op jit(solution)/shard_map/dot_general | solution.py:42
  361.9 74.3 %all-to-all-done.2 = bf16[16,24,7168]{2,1,0:T(8,128)(2,1)} async-done(((bf16[16,24,7168]{2,1,0:T(8,128)(2,1)}), bf16[16,24,7168]{2,1,0:T(8,128)(2,1)}, u32[]{:S(2)}, u32[]{:S(2)}) %all-to-all-start.2) | async-done | bytes 5505056 | tf_op jit(solution)/shard_map/all_to_all | solution.py:84
  436.2 19.7 %scatter_custom_fusion.2 = f32[257,7168]{1,0:T(8,128)} fusion(s32[384]{0:T(512)S(1)} %compare_select_fusion.1, bf16[384,7168]{1,0:T(8,128)(2,1)} %bitcast.16, f32[]{:T(128)} %constant.14.clone.1), kind=kCustom, calls=%fused_computation.5 | custom fusion | flops 5505024 | bytes 12873732 | tf_op jit(solution)/shard_map/scatter-add | solution.py:54
  455.9 5.4 %slice.31 = bf16[256,7168]{1,0:T(8,128)(2,1)} slice(f32[257,7168]{1,0:T(8,128)} %scatter_custom_fusion.2), slice={[0:256], [0:7168]} | slice | bytes 7340032 | tf_op jit(solution)/shard_map/slice | solution.py:56
  (30 shorter events, 5.9 us)
Async XLA Ops:
  0.6 142.4 %copy-start = (bf16[1,7168,128]{2,1,0:T(8,128)(2,1)S(1)}, bf16[1,7168,128]{2,1,0:T(8,128)(2,1)}, u32[]{:S(2)}) copy-start(bf16[1,7168,128]{2,1,0:T(8,128)(2,1)} %param.11) | copy-start | bytes 5505028
  37.4 7.2 %copy-start.3 = (f32[256,8]{0,1:T(8,128)S(1)}, f32[256,8]{0,1:T(8,128)}, u32[]{:S(2)}) copy-start(f32[256,8]{0,1:T(8,128)} %param.10) | copy-start | bytes 24580
  37.4 98.1 %all-to-all-start.1 = ((bf16[16,24,7168]{2,1,0:T(8,128)(2,1)}), bf16[16,24,7168]{2,1,0:T(8,128)(2,1)}, u32[]{:S(2)}, u32[]{:S(2)}) async-start(bf16[16,24,7168]{2,1,0:T(8,128)(2,1)} %bitcast.63), calls=%async_computation.1 | async-start | bytes 11010048 | tf_op jit(solution)/shard_map/all_to_all | solution.py:73
  135.5 74.7 %all-to-all-start = ((bf16[16,24,7168]{2,1,0:T(8,128)(2,1)}), bf16[16,24,7168]{2,1,0:T(8,128)(2,1)}, u32[]{:S(2)}, u32[]{:S(2)}) async-start(bf16[16,24,7168]{2,1,0:T(8,128)(2,1)} %fusion.2), calls=%async_computation | async-start | bytes 11010048 | tf_op jit(solution)/shard_map/all_to_all | solution.py:74
  143.1 4.3 copy-start.1
  214.9 1.6 copy-start.2
  339.1 97.1 %all-to-all-start.2 = ((bf16[16,24,7168]{2,1,0:T(8,128)(2,1)}), bf16[16,24,7168]{2,1,0:T(8,128)(2,1)}, u32[]{:S(2)}, u32[]{:S(2)}) async-start(bf16[16,24,7168]{2,1,0:T(8,128)(2,1)} %all-reduce.3), calls=%async_computation.2 | async-start | bytes 11010048 | tf_op jit(solution)/shard_map/all_to_all | solution.py:84
where the time goes:
time: 470 us; the launch traced here: 462 us
  waiting for transfers between devices  188 us (40%)
  blocking collectives  117 us (25%)
  local copies, waits for them, and re-layouts  64.4 us (14%)
  matrix products  36.4 us (8%)
  other arithmetic  32.8 us (7%)
  starting transfers between devices  21.7 us (5%)
    psum x1, blocking collectives, per_device(): whole = lax.psum(partial_rows, 'grp').astype(jnp.bfloat16)  117 us
    all_to_all x1, waiting for transfers between devices, per_device(): lax.all_to_all(whole, 'ep', split_axis=0, concat_axis=0, tiled=True)  74.3 us
    all_to_all x1, waiting for transfers between devices, per_device(): lax.all_to_all(send_c, 'ep', split_axis=0, concat_axis=0, tiled=True)  58.6 us
    all_to_all x1, waiting for transfers between devices, per_device(): lax.all_to_all(send_x, 'ep', split_axis=0, concat_axis=0, tiled=True)  55.3 us
    scatter-add x1, other arithmetic, combine_rows(): jnp.zeros((row_count + 1, flat_rows.shape[1]), jnp.float32).at[slot_token]  19.7 us
    gather x1, local copies, waits for them, and re-layouts, per_device(): pad_cotangent[slot_token].astype(jnp.float32)  15.8 us
    gather x1, local copies, waits for them, and re-layouts, per_device(): send_x = pad_tokens[slot_token].reshape(groups, MOST, features)  15.8 us
  transfers between devices with their start and end apart: 3, of which 3 were waited for; matrix products, arithmetic and copies ran while one was open for 13% of the time, Pallas kernels for 0%

commit v1 on v0

v1 whole, which is shorter than its diff:
```python
import functools

import jax
import jax.numpy as jnp
from jax import lax
from jax.experimental import pallas as pl
from jax.experimental.pallas import tpu as pltpu
from jax.sharding import PartitionSpec as P

BF = jnp.bfloat16
F32 = jnp.float32
MESH = pl.DeviceIdType.MESH

N = 16
SIDE = 4
T = 256
HID = 128
D = 7168
H = D // 2
W = 512
U = W // 2
NU = H // W
NG = 4
ND = NU - NG
R16 = N * 16
R8 = N * 8
R = R16 + R8
BLK = 48


def mm(a, b, ca=1, cb=0):
    return lax.dot_general(a, b, (((ca,), (cb,)), ((), ())), preferred_element_type=F32)


def pack(dst, g):
    g16 = g[:R16].reshape(N, 16, W)
    dst[:, 0:16, :] = g16[:, :, :U].astype(BF)
    dst[:, 16:32, :] = g16[:, :, U:].astype(BF)
    g8 = g[R16:].reshape(N, 8, W)
    dst[:, 32:48, :] = jnp.concatenate([g8[:, :, :U], g8[:, :, U:]], axis=1).astype(BF)


def body(
    tok, cot, ids, gs, gw, uw, dw,
    o_tok, o_gate, o_up, o_down,
    tokv, pm, q16, q8a, q8b, gate_col,
    send_a, recv_a, xm, wgu, wd, acc_gu, acc_h, accr_gu, accr_h, hid, g2,
    send_c, recv_c, zp, zr1, zs, zk, zr2, fin, dwgu, dwd,
    tok_sem, w_sem, ws_sem, wr_sem, as_sem, ar_sem, z1s_sem, z1r_sem, z2s_sem, z2r_sem,
    bs_sem, br_sem, cs_sem, cr_sem,
    s1s_sem, s1r_sem, s2s_sem, s2r_sem, g1s_sem, g1r_sem, g2s_sem, g2r_sem,
    ol_sem, os_sem, or_sem, dl_sem, ds_sem, dr_sem,
):
    g = lax.axis_index("grp")
    e = lax.axis_index("ep")
    z, c = g // 2, g % 2
    x, y = e // SIDE, e % SIDE
    other = 1 - c
    za = z + 1 - 2 * (z % 2)
    zb = 3 - z
    zo = 3 - za
    first = (za, zb)
    second = (zb, za)
    sib = (2 * z + other, e)

    def at_z(zz):
        return (2 * zz + c, e)

    def peer(k):
        return ((x + k // SIDE) % SIDE) * SIDE + (y + k % SIDE) % SIDE

    def remote(src, dst, ss, rs, dev):
        return pltpu.make_async_remote_copy(
            src_ref=src, dst_ref=dst, send_sem=ss, recv_sem=rs, device_id=dev, device_id_type=MESH
        )

    def mult(v, m):
        return pl.multiple_of(v, m)

    def unit_of(l):
        return z if l == 0 else NG + l - 1

    def load(a, l):
        src = (tok, cot)[a]
        return pltpu.make_async_copy(
            src.at[:, pl.ds(mult(c * H + unit_of(l) * W, W), W)], tokv.at[a, l], tok_sem.at[a, l]
        )

    for l in range(1 + ND):
        for a in range(2):
            load(a, l).start()

    my_half = mult(c * H, H)
    own_w = [
        pltpu.make_async_copy(gw.at[0, pl.ds(my_half, H)], wgu.at[c], w_sem.at[0]),
        pltpu.make_async_copy(uw.at[0, pl.ds(my_half, H)], wgu.at[2 + c], w_sem.at[1]),
        pltpu.make_async_copy(
            dw.at[0, :, pl.ds(my_half, H)], wd.at[pl.ds(mult(c * HID, HID), HID)], w_sem.at[2]
        ),
    ]
    for cp in own_w:
        cp.start()

    bar = pltpu.get_barrier_semaphore()

    def greet(k, carry):
        pl.semaphore_signal(bar, inc=1, device_id=(g, peer(k)), device_id_type=MESH)
        return carry

    lax.fori_loop(1, N, greet, 0)
    for dev in (at_z(za), at_z(zb), sib):
        pl.semaphore_signal(bar, inc=1, device_id=dev, device_id_type=MESH)

    idf = ids[...].astype(F32)
    e_col = jnp.min(idf, axis=1, keepdims=True)
    e_row = jnp.transpose(jnp.broadcast_to(e_col, (T, 128)))[0:1, :]
    gate_col[...] = jnp.sum(jnp.where(idf < N, gs[...], 0.0), axis=1, keepdims=True)
    sub = lax.broadcasted_iota(jnp.int32, (T, T), 0)
    lane = lax.broadcasted_iota(jnp.int32, (T, T), 1)
    same = e_col == e_row
    rank_row = jnp.sum(jnp.where(same & (sub < lane), 1.0, 0.0), axis=0, keepdims=True)
    rank_col = jnp.sum(jnp.where(same & (lane < sub), 1.0, 0.0), axis=1, keepdims=True)

    def onehot(test):
        return jnp.where(test, 1.0, 0.0).astype(BF)

    sf = lax.broadcasted_iota(jnp.int32, (R16, T), 0)
    pm[:R16, :] = onehot(((sf // 16).astype(F32) == e_row) & ((sf % 16).astype(F32) == rank_row))
    s8 = lax.broadcasted_iota(jnp.int32, (R8, T), 0)
    pm[R16:, :] = onehot(((s8 // 8).astype(F32) == e_row) & ((s8 % 8 + 16).astype(F32) == rank_row))
    of_e = (lane // 16).astype(F32) == e_col
    j16 = lane % 16
    q16[...] = onehot(of_e & (j16.astype(F32) == rank_col))
    late = of_e & ((j16 % 8 + 16).astype(F32) == rank_col)
    q8a[...] = onehot(late & (j16 < 8))
    q8b[...] = onehot(late & (j16 >= 8))

    pl.semaphore_wait(bar, N - 1 + 3)

    their_half = mult(other * H, H)
    sib_w = [
        remote(gw.at[0, pl.ds(their_half, H)], wgu.at[c], ws_sem.at[0], wr_sem.at[0], sib),
        remote(uw.at[0, pl.ds(their_half, H)], wgu.at[2 + c], ws_sem.at[1], wr_sem.at[1], sib),
        remote(
            dw.at[0, :, pl.ds(their_half, H)],
            wd.at[pl.ds(mult(c * HID, HID), HID)],
            ws_sem.at[2], wr_sem.at[2], sib,
        ),
    ]

    for l in range(1 + ND):
        for a in range(2):
            load(a, l).wait()
            u = unit_of(l)
            src = tokv[a, l]
            if a == 1:
                src = (gate_col[...] * src.astype(F32)).astype(BF)
            pack(send_a.at[a, l], mm(pm[...], src))
            recv_a[a, u, e] = send_a[a, l, e]

            def post(k, carry, a=a, l=l, u=u):
                dst = peer(k)
                remote(
                    send_a.at[a, l, dst], recv_a.at[a, u, e], as_sem.at[a, l], ar_sem.at[a, l], (g, dst)
                ).start()
                return carry

            lax.fori_loop(1, N, post, 0)
        if l == 0:
            for cp in sib_w:
                cp.start()

    def arrived(a, l):
        blocks = recv_a.at[a, unit_of(l), pl.ds(0, N - 1)]
        return remote(blocks, blocks, as_sem.at[a, l], ar_sem.at[a, l], sib)

    acc_gu[...] = jnp.zeros_like(acc_gu)
    acc_h[...] = jnp.zeros_like(acc_h)

    def process(a, u):
        cols = pl.ds(mult(u * W, W), W)
        r = recv_a[a, u]
        late8 = r[:, 32:48, :].astype(F32)
        xa = r[:, 0:16, :].reshape(R16, U)
        xb = r[:, 16:32, :].reshape(R16, U)
        ya = late8[:, 0:8, :].reshape(R8, U).astype(BF)
        yb = late8[:, 8:16, :].reshape(R8, U).astype(BF)
        left, right = pl.ds(mult(u * W, U), U), pl.ds(mult(u * W + U, U), U)
        xm[a, :R16, left] = xa
        xm[a, R16:, left] = ya
        xm[a, :R16, right] = xb
        xm[a, R16:, right] = yb
        rows = xm[a, :, cols]
        if a == 0:
            w = jnp.concatenate([wgu[i, cols, :] for i in range(4)], axis=1)
            acc_gu[...] += mm(rows, w)
        else:
            acc_h[...] += mm(rows, wd[:, cols], 1, 1)

    def step1(a):
        blk = recv_a.at[a, z]
        return remote(blk, blk, z1s_sem.at[a], z1r_sem.at[a], at_z(first[a]))

    def step2(a, i):
        blk = recv_a.at[a, (z, first[a])[i]]
        return remote(blk, blk, z2s_sem.at[a, i], z2r_sem.at[a, i], at_z(second[a]))

    for a in range(2):
        arrived(a, 0).wait_recv()
        step1(a).start()
        step2(a, 0).start()
    for i in range(3):
        own_w[i].wait()
        sib_w[i].wait_recv()
    for a in range(2):
        process(a, z)
    for a in range(2):
        step1(a).wait_recv()
        step2(a, 1).start()
    for a in range(2):
        process(a, first[a])

    def direct(l, carry):
        for a in range(2):
            blocks = recv_a.at[a, NG + l - 1, pl.ds(0, N - 1)]
            remote(blocks, blocks, as_sem.at[a, l], ar_sem.at[a, l], sib).wait_recv()
            process(a, NG + l - 1)
        return carry

    lax.fori_loop(1, 1 + ND, direct, 0)
    for a in range(2):
        step2(a, 0).wait_recv()
        process(a, second[a])
    b_gu = remote(acc_gu, accr_gu, bs_sem.at[0], br_sem.at[0], sib)
    b_h = remote(acc_h, accr_h, bs_sem.at[1], br_sem.at[1], sib)
    step2(0, 1).wait_recv()
    process(0, zo)
    b_gu.start()
    step2(1, 1).wait_recv()
    process(1, zo)
    b_h.start()
    b_gu.wait_recv()
    b_h.wait_recv()

    RB = 64

    def act(i, carry):
        rows = pl.ds(mult(i * RB, RB), RB)
        gu = acc_gu[rows, :] + accr_gu[rows, :]
        gh = acc_h[rows, :] + accr_h[rows, :]
        gp, up = gu[:, : 2 * HID], gu[:, 2 * HID :]
        sg = jax.nn.sigmoid(gp)
        silu = gp * sg
        hid[rows, :] = (silu * up).astype(BF)
        g2[rows, : 2 * HID] = (gh * up * sg * (1.0 + gp * (1.0 - sg))).astype(BF)
        g2[rows, 2 * HID :] = (gh * silu).astype(BF)
        return carry

    lax.fori_loop(0, R // RB, act, 0)

    def row_grad(j, carry):
        cols = pl.ds(mult(j * W, W), W)
        w = jnp.concatenate([wgu[i, cols, :] for i in range(4)], axis=1)
        pack(send_c.at[j], mm(g2[...], w, 1, 1))
        recv_c[j, e] = send_c[j, e]

        def post(k, inner):
            dst = peer(k)
            remote(send_c.at[j, dst], recv_c.at[j, e], cs_sem.at[j], cr_sem.at[j], (g, dst)).start()
            return inner

        lax.fori_loop(1, N, post, 0)
        return carry

    lax.fori_loop(0, NU, row_grad, 0)

    bit1 = (((z + 1) // 2) % 2, z // 2)
    bit2 = (z // 2, z % 2)

    def rs1(j, p):
        off = mult((1 - bit1[p]) * 128, 128)
        return remote(
            zp.at[j, p, pl.ds(off, 128)], zr1.at[j, p], s1s_sem.at[j, p], s1r_sem.at[j, p], at_z(first[p])
        )

    def rs2(j, p):
        return remote(zs.at[j, p], zr2.at[j, p], s2s_sem.at[j, p], s2r_sem.at[j, p], at_z(second[p]))

    def ag1(j, p):
        blk = fin.at[j, p, pl.ds(mult(bit1[p] * 128 + bit2[p] * 64, 64), 64)]
        return remote(blk, blk, g1s_sem.at[j, p], g1r_sem.at[j, p], at_z(second[p]))

    def ag2(j, p):
        blk = fin.at[j, p, pl.ds(mult(bit1[p] * 128, 128), 128)]
        return remote(blk, blk, g2s_sem.at[j, p], g2r_sem.at[j, p], at_z(first[p]))

    def out_cols(j, p):
        return pl.ds(mult(c * H + j * W + p * U, U), U)

    def out_local(j, p):
        return pltpu.make_async_copy(fin.at[j, p], o_tok.at[:, out_cols(j, p)], ol_sem.at[j, p])

    def out_sib(j, p):
        return remote(fin.at[j, p], o_tok.at[:, out_cols(j, p)], os_sem.at[j, p], or_sem.at[j, p], sib)

    def grads_out(j):
        rows = pl.ds(mult(j * W, W), W)
        orow = pl.ds(mult(c * H + j * W, W), W)
        local, far = [], []
        for i, out in enumerate((o_gate, o_up)):
            local.append(pltpu.make_async_copy(dwgu.at[2 * i + c, rows], out.at[0, orow], dl_sem.at[j, i]))
            far.append(remote(dwgu.at[2 * i + other, rows], out.at[0, orow], ds_sem.at[j, i], dr_sem.at[j, i], sib))
        mine, yours = pl.ds(mult(c * HID, HID), HID), pl.ds(mult(other * HID, HID), HID)
        local.append(pltpu.make_async_copy(dwd.at[mine, rows], o_down.at[0, :, orow], dl_sem.at[j, 2]))
        far.append(remote(dwd.at[yours, rows], o_down.at[0, :, orow], ds_sem.at[j, 2], dr_sem.at[j, 2], sib))
        return local, far

    def pipe(t, carry):
        @pl.when(t < NU)
        def _():
            blocks = recv_c.at[t, pl.ds(0, N - 1)]
            remote(blocks, blocks, cs_sem.at[t], cr_sem.at[t], sib).wait_recv()
            r = recv_c[t]
            r8 = r[:, 32:48, :].reshape(R16, U)
            for p in range(2):
                r16 = r[:, 16 * p : 16 * p + 16, :].reshape(R16, U)
                zp[t, p] = (mm(q16[...], r16) + mm((q8a, q8b)[p][...], r8)).astype(BF)
                rs1(t, p).start()

        @pl.when((t >= 1) & (t < NU + 1))
        def _():
            j = t - 1
            for p in range(2):
                rs1(j, p).wait_recv()
                base = bit1[p] * 128
                keep = pl.ds(mult(base + bit2[p] * 64, 64), 64)
                give = pl.ds(mult(base + (1 - bit2[p]) * 64, 64), 64)
                rk = pl.ds(mult(bit2[p] * 64, 64), 64)
                rg = pl.ds(mult((1 - bit2[p]) * 64, 64), 64)
                zs[j, p] = (zp[j, p, give, :].astype(F32) + zr1[j, p, rg, :].astype(F32)).astype(BF)
                rs2(j, p).start()
                zk[j, p] = zp[j, p, keep, :].astype(F32) + zr1[j, p, rk, :].astype(F32)

        @pl.when((t >= 2) & (t < NU + 2))
        def _():
            j = t - 2
            for p in range(2):
                rs2(j, p).wait_recv()
                rows = pl.ds(mult(bit1[p] * 128 + bit2[p] * 64, 64), 64)
                fin[j, p, rows, :] = (zk[j, p] + zr2[j, p].astype(F32)).astype(BF)
                ag1(j, p).start()

        @pl.when((t >= 3) & (t < NU + 3))
        def _():
            for p in range(2):
                ag1(t - 3, p).wait_recv()
                ag2(t - 3, p).start()

        @pl.when(t >= 4)
        def _():
            for p in range(2):
                ag2(t - 4, p).wait_recv()
                out_local(t - 4, p).start()
                out_sib(t - 4, p).start()

        @pl.when(t < NU)
        def _():
            cols = pl.ds(mult(t * W, W), W)
            d1 = mm(xm[0, :, cols], g2[...], 0, 0)
            for i in range(4):
                dwgu[i, cols, :] = d1[:, i * HID : (i + 1) * HID].astype(BF)
            dwd[:, cols] = mm(hid[...], xm[1, :, cols], 0, 0).astype(BF)
            local, far = grads_out(t)
            for cp in local + far:
                cp.start()

        return carry

    lax.fori_loop(0, NU + 4, pipe, 0)

    for a in range(2):
        for l in range(1 + ND):
            arrived(a, l).wait_send()
        step1(a).wait_send()
        for i in range(2):
            step2(a, i).wait_send()
    for i in range(3):
        sib_w[i].wait_send()
    b_gu.wait_send()
    b_h.wait_send()

    def drain(j, carry):
        blocks = send_c.at[j, pl.ds(0, N - 1)]
        remote(blocks, blocks, cs_sem.at[j], cr_sem.at[j], sib).wait_send()
        for p in range(2):
            for cp in (rs1(j, p), rs2(j, p), ag1(j, p), ag2(j, p), out_sib(j, p)):
                cp.wait_send()
            out_local(j, p).wait()
            out_sib(j, p).wait_recv()
        local, far = grads_out(j)
        for cp in local:
            cp.wait()
        for cp in far:
            cp.wait()
        return carry

    lax.fori_loop(0, NU, drain, 0)


def per_device(tokens, cotangent, expert_ids, gate_scores, gate_weight, up_weight, down_weight):
    def sems(*shape):
        return pltpu.SemaphoreType.DMA(shape)

    anyspace = pl.BlockSpec(memory_space=pl.ANY)
    vmem = pl.BlockSpec(memory_space=pltpu.VMEM)
    scratch = [
        pltpu.VMEM((2, 1 + ND, T, W), BF),
        pltpu.VMEM((R, T), BF),
        pltpu.VMEM((T, R16), BF),
        pltpu.VMEM((T, R16), BF),
        pltpu.VMEM((T, R16), BF),
        pltpu.VMEM((T, 1), F32),
        pltpu.VMEM((2, 1 + ND, N, BLK, U), BF),
        pltpu.VMEM((2, NU, N, BLK, U), BF),
        pltpu.VMEM((2, R, H), BF),
        pltpu.VMEM((4, H, HID), BF),
        pltpu.VMEM((2 * HID, H), BF),
        pltpu.VMEM((R, 4 * HID), F32),
        pltpu.VMEM((R, 2 * HID), F32),
        pltpu.VMEM((R, 4 * HID), F32),
        pltpu.VMEM((R, 2 * HID), F32),
        pltpu.VMEM((R, 2 * HID), BF),
        pltpu.VMEM((R, 4 * HID), BF),
        pltpu.VMEM((NU, N, BLK, U), BF),
        pltpu.VMEM((NU, N, BLK, U), BF),
        pltpu.VMEM((NU, 2, T, U), BF),
        pltpu.VMEM((NU, 2, 128, U), BF),
        pltpu.VMEM((NU, 2, 64, U), BF),
        pltpu.VMEM((NU, 2, 64, U), F32),
        pltpu.VMEM((NU, 2, 64, U), BF),
        pltpu.VMEM((NU, 2, T, U), BF),
        pltpu.VMEM((4, H, HID), BF),
        pltpu.VMEM((2 * HID, H), BF),
        sems(2, 1 + ND), sems(3), sems(3), sems(3),
        sems(2, 1 + ND), sems(2, 1 + ND),
        sems(2), sems(2), sems(2, 2), sems(2, 2),
        sems(2), sems(2), sems(NU), sems(NU),
        sems(NU, 2), sems(NU, 2), sems(NU, 2), sems(NU, 2),
        sems(NU, 2), sems(NU, 2), sems(NU, 2), sems(NU, 2),
        sems(NU, 2), sems(NU, 2), sems(NU, 2),
        sems(NU, 3), sems(NU, 3), sems(NU, 3),
    ]
    return tuple(
        pl.pallas_call(
            body,
            out_shape=[
                jax.ShapeDtypeStruct((T, D), BF),
                jax.ShapeDtypeStruct((1, D, HID), BF),
                jax.ShapeDtypeStruct((1, D, HID), BF),
                jax.ShapeDtypeStruct((1, HID, D), BF),
            ],
            in_specs=[anyspace, anyspace, vmem, vmem, anyspace, anyspace, anyspace],
            out_specs=[anyspace] * 4,
            scratch_shapes=scratch,
            compiler_params=pltpu.CompilerParams(
                collective_id=0, has_side_effects=True, vmem_limit_bytes=60 * 1024 * 1024
            ),
            cost_estimate=pl.CostEstimate(flops=6_000_000_000, bytes_accessed=20_000_000, transcendentals=100_000),
        )(tokens, cotangent, expert_ids, gate_scores, gate_weight, up_weight, down_weight)
    )


def solution(mesh):
    placed = (
        P("ep", None),
        P("ep", None),
        P("ep", None),
        P("ep", None),
        P("ep", None, "grp"),
        P("ep", None, "grp"),
        P("ep", "grp", None),
    )
    return jax.shard_map(
        per_device,
        mesh=mesh,
        in_specs=placed,
        out_specs=(P("ep", None), P("ep", None, "grp"), P("ep", None, "grp"), P("ep", "grp", None)),
        check_vma=False,
    )
```

time: 470 us -> 119 us (0.25)
  the two profiles are of different devices: /device:TPU:28 before, /device:TPU:1 now
where the time goes in v1:
time: 119 us; the launch traced here: 118 us
  Pallas kernels  105 us (88%)
  local copies, waits for them, and re-layouts  12.8 us (11%)
    pallas_call x1, Pallas kernels, per_device(): pl.pallas_call(body, out_shape=[jax.ShapeDtypeStruct((T, D), BF), jax.Sha...  105 us
    unnamed x12, local copies, waits for them, and re-layouts  12.8 us

profile of v1, /device:TPU:1, one launch (start us, length us, event | category | flops | bytes accessed | tf_op | source)
XLA Modules:
  0.0 118.4 jit_solution(12248927688145983334)
XLA Ops:
  0.6 1.5 %copy.11.ids = s32[256,8]{1,0:T(8,128)} copy(s32[256,8]{0,1:T(8,128)} %param.9) | data formatting | bytes 16384 | tf_op args[2]
  2.1 1.5 %copy.12.gs = f32[256,8]{1,0:T(8,128)} copy(f32[256,8]{0,1:T(8,128)} %param.10) | data formatting | bytes 16384 | tf_op args[3]
  3.6 105.0 %shard_map.102 = (bf16[256,7168]{1,0:T(8,128)(2,1)}, bf16[1,7168,128]{2,1,0:T(8,128)(2,1)}, bf16[1,7168,128]{2,1,0:T(8,128)(2,1)}, bf16[1,128,7168]{2,1,0:T(8,128)(2,1)}) custom-call(bf16[256,7168]{1,0:T(8,128)(2,1)} %tok.1, bf16[256,7168]{1,0:T(8,128)(2,1)} %cot.1, s32[256,8]{1,0:T(8,128)} %copy.11.ids, f32[256,8]{1,0:T(8,128)} %copy.12.gs, ...), custom_call_target="tpu_custom_call" | custom-call | flops 6000000000 | bytes 20000000 | tf_op jit(solution)/shard_map/pallas_call | solution.py:454
  108.6 0.0 copy-start.2
  108.6 4.2 %copy.17 = bf16[256,7168]{1,0:T(8,128)(2,1)} copy(bf16[256,7168]{1,0:T(8,128)(2,1)} %get-tuple-element.8) | data formatting | bytes 7340032
  112.8 0.0 copy-done.2
  112.8 0.0 copy-start.1
  112.8 1.2 %copy.18 = bf16[1,7168,128]{2,1,0:T(8,128)(2,1)} copy(bf16[1,7168,128]{2,1,0:T(8,128)(2,1)S(1)} %copy-done.2) | data formatting | bytes 3670016
  114.1 0.9 copy-done.1
  115.0 0.0 copy-start
  115.0 1.2 %copy.19 = bf16[1,7168,128]{2,1,0:T(8,128)(2,1)} copy(bf16[1,7168,128]{2,1,0:T(8,128)(2,1)S(1)} %copy-done.1) | data formatting | bytes 3670016
  116.2 0.9 copy-done
  117.2 1.2 %copy.20 = bf16[1,128,7168]{2,1,0:T(8,128)(2,1)} copy(bf16[1,128,7168]{2,1,0:T(8,128)(2,1)S(1)} %copy-done) | data formatting | bytes 3670016
Async XLA Ops:
  108.6 4.3 %copy-start.2 = (bf16[1,7168,128]{2,1,0:T(8,128)(2,1)S(1)}, bf16[1,7168,128]{2,1,0:T(8,128)(2,1)}, u32[]{:S(2)}) copy-start(bf16[1,7168,128]{2,1,0:T(8,128)(2,1)} %get-tuple-element.9) | copy-start | bytes 5505028
  112.8 2.2 %copy-start.1 = (bf16[1,7168,128]{2,1,0:T(8,128)(2,1)S(1)}, bf16[1,7168,128]{2,1,0:T(8,128)(2,1)}, u32[]{:S(2)}) copy-start(bf16[1,7168,128]{2,1,0:T(8,128)(2,1)} %get-tuple-element.10) | copy-start | bytes 5505028
  115.0 2.2 %copy-start = (bf16[1,128,7168]{2,1,0:T(8,128)(2,1)S(1)}, bf16[1,128,7168]{2,1,0:T(8,128)(2,1)}, u32[]{:S(2)}) copy-start(bf16[1,128,7168]{2,1,0:T(8,128)(2,1)} %get-tuple-element.11) | copy-start | bytes 5505028

commit v2 on v1

v2 whole, which is shorter than its diff:
```python
import functools

import jax
import jax.numpy as jnp
from jax import lax
from jax.experimental import pallas as pl
from jax.experimental.pallas import tpu as pltpu
from jax.sharding import PartitionSpec as P

BF = jnp.bfloat16
F32 = jnp.float32
MESH = pl.DeviceIdType.MESH

N = 16
SIDE = 4
T = 256
HID = 128
D = 7168
H = D // 2
W = 512
U = 128
C = 2 * U
NU = H // W
NA = H // C
NP = 5
ND = NA - 2 * NP
R16 = N * 16
R8 = N * 8
R = R16 + R8
BLK = 48
OFFS = (
    (2, 2), (2, 3), (3, 2), (2, 1), (1, 2), (2, 0), (0, 2), (3, 1),
    (1, 3), (3, 3), (1, 1), (3, 0), (0, 3), (1, 0), (0, 1),
)
RB = 128
LAG = 2


def mm(a, b, ca=1, cb=0):
    return lax.dot_general(a, b, (((ca,), (cb,)), ((), ())), preferred_element_type=F32)


def pack(dst, g):
    g16 = g[:R16].reshape(N, 16, C)
    dst[:, 0:16, :] = g16[:, :, :U].astype(BF)
    dst[:, 16:32, :] = g16[:, :, U:].astype(BF)
    g8 = g[R16:].reshape(N, 8, C)
    dst[:, 32:48, :] = jnp.concatenate([g8[:, :, :U], g8[:, :, U:]], axis=1).astype(BF)


def body(
    tok, cot, ids, gs, gw, uw, dw,
    o_tok, o_gate, o_up, o_down,
    tokv, tokd, pm, q16, q8a, q8b, scale, gate_col,
    send_a, send_d, recv_a, xm, wgu, wd, acc_gu, acc_h, accr_gu, accr_h, hid, g2,
    pk, rsb, send_c, recv_c, zp, zr, fin, dwgu, dwd,
    tok_sem, tokd_sem, w_sem, ws_sem, wr_sem, as_sem, ar_sem, ds_a_sem, dr_a_sem, z1s_sem, z1r_sem, z2s_sem, z2r_sem,
    bs_sem, br_sem, ps_sem, pr_sem, cs_sem, cr_sem, xs_sem, xr_sem, gs_sem, gr_sem,
    ol_sem, os_sem, or_sem, dl_sem, ds_sem, dr_sem,
):
    g = lax.axis_index("grp")
    e = lax.axis_index("ep")
    z, c = g // 2, g % 2
    x, y = e // SIDE, e % SIDE
    other = 1 - c
    za = z + 1 - 2 * (z % 2)
    zb = 3 - z
    zo = 3 - za
    sib = (2 * z + other, e)

    def first(i):
        return za + (zb - za) * (i % 2)

    def second(i):
        return zb + (za - zb) * (i % 2)

    def at_z(zz):
        return (2 * zz + c, e)

    def peer(k):
        dx, dy = OFFS[k]
        if dx != dy:
            dx, dy = dx * other + dy * c, dy * other + dx * c
        return ((x + dx) % SIDE) * SIDE + (y + dy) % SIDE

    def remote(src, dst, ss, rs, dev):
        return pltpu.make_async_remote_copy(
            src_ref=src, dst_ref=dst, send_sem=ss, recv_sem=rs, device_id=dev, device_id_type=MESH
        )

    def mult(v, m):
        return pl.multiple_of(v, m)

    bar = pltpu.get_barrier_semaphore()
    for k in range(N - 1):
        pl.semaphore_signal(bar, inc=1, device_id=(g, peer(k)), device_id_type=MESH)
    for dev in (at_z(za), at_z(zb), sib):
        pl.semaphore_signal(bar, inc=1, device_id=dev, device_id_type=MESH)

    def load(src):
        col = mult(c * H + (z % 2) * NP * C, C)
        return pltpu.make_async_copy(src.at[:, pl.ds(col, NP * C)], tokv, tok_sem)

    def load_d(a):
        col = mult(c * H + 2 * NP * C, C)
        return pltpu.make_async_copy((tok, cot)[a].at[:, pl.ds(col, ND * C)], tokd.at[a], tokd_sem.at[a])

    @pl.when(z < 2)
    def _():
        load(tok).start()

    @pl.when(z >= 2)
    def _():
        load(cot).start()

    for a in range(2):
        load_d(a).start()

    my_half = mult(c * H, H)
    own_w = [
        pltpu.make_async_copy(gw.at[0, pl.ds(my_half, H)], wgu.at[c], w_sem.at[0]),
        pltpu.make_async_copy(uw.at[0, pl.ds(my_half, H)], wgu.at[2 + c], w_sem.at[1]),
        pltpu.make_async_copy(
            dw.at[0, :, pl.ds(my_half, H)], wd.at[pl.ds(mult(c * HID, HID), HID)], w_sem.at[2]
        ),
    ]
    for cp in own_w:
        cp.start()

    def column(row):
        return jnp.transpose(jnp.broadcast_to(row, (128, T)))[:, 0:1]

    idf = ids[...].astype(F32)
    e_row = jnp.min(idf, axis=0, keepdims=True)
    e_col = column(e_row)
    sub = lax.broadcasted_iota(jnp.int32, (T, T), 0)
    lane = lax.broadcasted_iota(jnp.int32, (T, T), 1)
    before = jnp.where(sub < lane, jnp.where(e_col == e_row, 1.0, 0.0), 0.0)
    rank_row = jnp.sum(before, axis=0, keepdims=True)
    valid = e_row < N
    slot16 = jnp.where(valid & (rank_row < 16), e_row * 16 + rank_row, -1.0)
    slot8 = jnp.where(valid & (rank_row >= 16), e_row * 8 + (rank_row - 16), -1.0)

    def onehot(test):
        return jnp.where(test, 1.0, 0.0).astype(BF)

    subf = sub.astype(F32)
    pm[:R16, :] = onehot(subf == slot16)
    pm[R16:, :] = onehot(subf[:R8] == slot8)
    gate_row = jnp.sum(jnp.where(idf < N, gs[...], 0.0), axis=0, keepdims=True)
    gate_col[...] = column(gate_row)
    scale[...] = column(jnp.where(z < 2, jnp.ones_like(gate_row), gate_row))

    pl.semaphore_wait(bar, N - 1 + 3)

    their_half = mult(other * H, H)
    sib_w = [
        remote(gw.at[0, pl.ds(their_half, H)], wgu.at[c], ws_sem.at[0], wr_sem.at[0], sib),
        remote(uw.at[0, pl.ds(their_half, H)], wgu.at[2 + c], ws_sem.at[1], wr_sem.at[1], sib),
        remote(
            dw.at[0, :, pl.ds(their_half, H)],
            wd.at[pl.ds(mult(c * HID, HID), HID)],
            ws_sem.at[2], wr_sem.at[2], sib,
        ),
    ]

    for cp in sib_w:
        cp.start()

    def spread(buf, n, ss, rs):
        recv_a[n, e] = buf[e]
        for k in range(N - 1):
            dst = peer(k)
            remote(buf.at[dst], recv_a.at[n, e], ss, rs, (g, dst)).start()

    def part_of(owner, i):
        return (owner // 2) * NA + (owner % 2) * NP + i

    def dispatch(i, carry):
        src = tokv[:, pl.ds(mult(i * C, C), C)]
        src = (scale[...] * src.astype(F32)).astype(BF)
        pack(send_a.at[i], mm(pm[...], src))
        spread(send_a.at[i], part_of(z, i), as_sem.at[i], ar_sem.at[i])
        return carry

    def dispatch_d(d):
        for a in range(2):
            src = tokd[a, :, pl.ds(mult(d * C, C), C)]
            if a == 1:
                src = (gate_col[...] * src.astype(F32)).astype(BF)
            pack(send_d.at[a, d], mm(pm[...], src))
            spread(send_d.at[a, d], a * NA + 2 * NP + d, ds_a_sem.at[a, d], dr_a_sem.at[a, d])

    load(tok).wait()
    lax.fori_loop(0, NP, dispatch, 0)
    for a in range(2):
        load_d(a).wait()

    lanef = lane.astype(F32)
    q16[...] = onehot(lanef == column(slot16))
    late_a = jnp.where(valid & (rank_row >= 16), e_row * 16 + (rank_row - 16), -16.0)
    q8a[...] = onehot(lanef == column(late_a))
    q8b[...] = onehot(lanef == column(late_a + 8))
    acc_gu[...] = jnp.zeros_like(acc_gu)
    acc_h[...] = jnp.zeros_like(acc_h)

    def arrived(i):
        blocks = recv_a.at[part_of(z, i), pl.ds(0, N - 1)]
        return remote(blocks, blocks, as_sem.at[i], ar_sem.at[i], sib)

    def arrived_d(a, d):
        blocks = recv_a.at[a * NA + 2 * NP + d, pl.ds(0, N - 1)]
        return remote(blocks, blocks, ds_a_sem.at[a, d], dr_a_sem.at[a, d], sib)

    def unpack(a, m):
        r = recv_a[a * NA + m]
        late8 = r[:, 32:48, :].astype(F32)
        left, right = pl.ds(mult(m * C, U), U), pl.ds(mult(m * C + U, U), U)
        xm[a, :R16, left] = r[:, 0:16, :].reshape(R16, U)
        xm[a, R16:, left] = late8[:, 0:8, :].reshape(R8, U).astype(BF)
        xm[a, :R16, right] = r[:, 16:32, :].reshape(R16, U)
        xm[a, R16:, right] = late8[:, 8:16, :].reshape(R8, U).astype(BF)

    def multiply(a, m):
        cols = pl.ds(mult(m * C, C), C)
        if a == 0:
            w = jnp.concatenate([wgu[k, cols, :] for k in range(4)], axis=1)
            acc_gu[...] += mm(xm[0, :, cols], w)
        else:
            acc_h[...] += mm(xm[1, :, cols], wd[:, cols], 1, 1)

    def process_of(owner, i):
        a, m = owner // 2, (owner % 2) * NP + i
        unpack(a, m)

        @pl.when(a == 0)
        def _():
            multiply(0, m)

        @pl.when(a == 1)
        def _():
            multiply(1, m)

    def process_d(d):
        for a in range(2):
            arrived_d(a, d).wait_recv()
            unpack(a, 2 * NP + d)
            multiply(a, 2 * NP + d)

    def step1(i):
        blk = recv_a.at[part_of(z, i)]
        return remote(blk, blk, z1s_sem.at[i], z1r_sem.at[i], at_z(first(i)))

    def step2(i, fwd):
        blk = recv_a.at[part_of(first(i), i) if fwd else part_of(z, i)]
        return remote(blk, blk, z2s_sem.at[i, fwd], z2r_sem.at[i, fwd], at_z(second(i)))

    dispatch_d(0)

    def gather1(i, carry):
        arrived(i).wait_recv()
        step1(i).start()
        step2(i, 0).start()

        @pl.when(i + 1 < ND)
        def _():
            dispatch_d(i + 1)

        return carry

    lax.fori_loop(0, NP, gather1, 0)
    for d in range(NP + 1, ND):
        dispatch_d(d)
    for k in range(3):
        own_w[k].wait()
        sib_w[k].wait_recv()

    def gather2(i, carry):
        step1(i).wait_recv()
        step2(i, 1).start()
        process_of(z, i)
        process_of(first(i), i)

        @pl.when(i < ND)
        def _():
            process_d(i)

        return carry

    lax.fori_loop(0, NP, gather2, 0)

    def gather3(i, carry):
        @pl.when(i + NP < ND)
        def _():
            process_d(i + NP)

        step2(i, 0).wait_recv()
        process_of(second(i), i)
        step2(i, 1).wait_recv()
        process_of(zo, i)
        return carry

    lax.fori_loop(0, NP, gather3, 0)

    def swap(i):
        rows = pl.ds(mult(i * RB, RB), RB)
        return (
            remote(acc_gu.at[rows], accr_gu.at[rows], bs_sem.at[0, i], br_sem.at[0, i], sib),
            remote(acc_h.at[rows], accr_h.at[rows], bs_sem.at[1, i], br_sem.at[1, i], sib),
        )

    for i in range(R // RB):
        for cp in swap(i):
            cp.start()

    def act(i, carry):
        rows = pl.ds(mult(i * RB, RB), RB)
        for cp in swap(i):
            cp.wait_recv()
        gu = acc_gu[rows, :] + accr_gu[rows, :]
        gh = acc_h[rows, :] + accr_h[rows, :]
        gp, up = gu[:, : 2 * HID], gu[:, 2 * HID :]
        sg = jax.nn.sigmoid(gp)
        silu = gp * sg
        hid[rows, :] = (silu * up).astype(BF)
        g2[rows, : 2 * HID] = (gh * up * sg * (1.0 + gp * (1.0 - sg))).astype(BF)
        g2[rows, 2 * HID :] = (gh * silu).astype(BF)
        return carry

    lax.fori_loop(0, R // RB, act, 0)

    def half(j):
        b = ((z + 1) // 2) % 2
        return b + (z // 2 - b) * (j % 2)

    def pair(j):
        return remote(pk.at[j, 1 - half(j)], rsb.at[j], ps_sem.at[j], pr_sem.at[j], at_z(first(j)))

    def row_grad(j, carry):
        cols = pl.ds(mult(j * W, W), W)
        w = jnp.concatenate([wgu[i, cols, :] for i in range(4)], axis=1)
        r = mm(g2[...], w, 1, 1)
        for h in range(2):
            pack(pk.at[j, h], r[:, h * C : (h + 1) * C])
        pair(j).start()
        return carry

    lax.fori_loop(0, NU, row_grad, 0)

    def back(j, carry):
        pair(j).wait_recv()
        send_c[j] = (pk[j, half(j)].astype(F32) + rsb[j].astype(F32)).astype(BF)
        recv_c[j, e] = send_c[j, e]
        for k in range(N - 1):
            dst = peer(k)
            remote(send_c.at[j, dst], recv_c.at[j, e], cs_sem.at[j], cr_sem.at[j], (g, dst)).start()
        return carry

    lax.fori_loop(0, NU, back, 0)

    def cross(j):
        return remote(zp.at[j], zr.at[j], xs_sem.at[j], xr_sem.at[j], at_z(second(j)))

    def whole(j):
        blk = fin.at[j, half(j)]
        return remote(blk, blk, gs_sem.at[j], gr_sem.at[j], at_z(first(j)))

    def out_cols(j, p):
        return pl.ds(mult(c * H + j * W + p * C, C), C)

    def out_local(j, p):
        return pltpu.make_async_copy(fin.at[j, p], o_tok.at[:, out_cols(j, p)], ol_sem.at[j, p])

    def out_sib(j, p):
        return remote(fin.at[j, p], o_tok.at[:, out_cols(j, p)], os_sem.at[j, p], or_sem.at[j, p], sib)

    def grads_out(j):
        rows = pl.ds(mult(j * W, W), W)
        orow = pl.ds(mult(c * H + j * W, W), W)
        local, far = [], []
        for i, out in enumerate((o_gate, o_up)):
            local.append(pltpu.make_async_copy(dwgu.at[2 * i + c, rows], out.at[0, orow], dl_sem.at[j, i]))
            far.append(remote(dwgu.at[2 * i + other, rows], out.at[0, orow], ds_sem.at[j, i], dr_sem.at[j, i], sib))
        mine, yours = pl.ds(mult(c * HID, HID), HID), pl.ds(mult(other * HID, HID), HID)
        local.append(pltpu.make_async_copy(dwd.at[mine, rows], o_down.at[0, :, orow], dl_sem.at[j, 2]))
        far.append(remote(dwd.at[yours, rows], o_down.at[0, :, orow], ds_sem.at[j, 2], dr_sem.at[j, 2], sib))
        return local, far

    def pipe(t, carry):
        @pl.when(t < NU)
        def _():
            blocks = recv_c.at[t, pl.ds(0, N - 1)]
            remote(blocks, blocks, cs_sem.at[t], cr_sem.at[t], sib).wait_recv()
            r = recv_c[t]
            r8 = r[:, 32:48, :].reshape(R16, U)
            for p in range(2):
                r16 = r[:, 16 * p : 16 * p + 16, :].reshape(R16, U)
                zp[t, :, p * U : (p + 1) * U] = (mm(q16[...], r16) + mm((q8a, q8b)[p][...], r8)).astype(BF)
            cross(t).start()

        @pl.when((t >= LAG) & (t < NU + LAG))
        def _():
            j = t - LAG
            cross(j).wait_recv()
            fin[j, half(j)] = (zp[j].astype(F32) + zr[j].astype(F32)).astype(BF)
            whole(j).start()

        @pl.when(t >= 2 * LAG)
        def _():
            whole(t - 2 * LAG).wait_recv()
            for p in range(2):
                out_local(t - 2 * LAG, p).start()
                out_sib(t - 2 * LAG, p).start()

        @pl.when(t < NU)
        def _():
            cols = pl.ds(mult(t * W, W), W)
            d1 = mm(xm[0, :, cols], g2[...], 0, 0)
            for i in range(4):
                dwgu[i, cols, :] = d1[:, i * HID : (i + 1) * HID].astype(BF)
            dwd[:, cols] = mm(hid[...], xm[1, :, cols], 0, 0).astype(BF)
            local, far = grads_out(t)
            for cp in local + far:
                cp.start()

        return carry

    lax.fori_loop(0, NU + 2 * LAG, pipe, 0)

    for i in range(3):
        sib_w[i].wait_send()
        for cp in swap(i):
            cp.wait_send()

    def drain_a(i, carry):
        arrived(i).wait_send()
        step1(i).wait_send()
        step2(i, 0).wait_send()
        step2(i, 1).wait_send()
        return carry

    lax.fori_loop(0, NP, drain_a, 0)
    for d in range(ND):
        for a in range(2):
            arrived_d(a, d).wait_send()

    def drain(j, carry):
        blocks = send_c.at[j, pl.ds(0, N - 1)]
        remote(blocks, blocks, cs_sem.at[j], cr_sem.at[j], sib).wait_send()
        for cp in (pair(j), cross(j), whole(j)):
            cp.wait_send()
        for p in range(2):
            out_local(j, p).wait()
            out_sib(j, p).wait()
        local, far = grads_out(j)
        for cp in local + far:
            cp.wait()
        return carry

    lax.fori_loop(0, NU, drain, 0)


def write_out(*refs):
    sem = refs[8]
    copies = [pltpu.make_async_copy(refs[i], refs[4 + i], sem.at[i]) for i in range(4)]
    for cp in copies:
        cp.start()
    for cp in copies:
        cp.wait()


def per_device(tokens, cotangent, expert_ids, gate_scores, gate_weight, up_weight, down_weight):
    def sems(*shape):
        return pltpu.SemaphoreType.DMA(shape)

    anyspace = pl.BlockSpec(memory_space=pl.ANY)
    vmem = pl.BlockSpec(memory_space=pltpu.VMEM)
    scratch = [
        pltpu.VMEM((T, NP * C), BF),
        pltpu.VMEM((2, T, ND * C), BF),
        pltpu.VMEM((R, T), BF),
        pltpu.VMEM((T, R16), BF),
        pltpu.VMEM((T, R16), BF),
        pltpu.VMEM((T, R16), BF),
        pltpu.VMEM((T, 1), F32),
        pltpu.VMEM((T, 1), F32),
        pltpu.VMEM((NP, N, BLK, U), BF),
        pltpu.VMEM((2, ND, N, BLK, U), BF),
        pltpu.VMEM((2 * NA, N, BLK, U), BF),
        pltpu.VMEM((2, R, H), BF),
        pltpu.VMEM((4, H, HID), BF),
        pltpu.VMEM((2 * HID, H), BF),
        pltpu.VMEM((R, 4 * HID), F32),
        pltpu.VMEM((R, 2 * HID), F32),
        pltpu.VMEM((R, 4 * HID), F32),
        pltpu.VMEM((R, 2 * HID), F32),
        pltpu.VMEM((R, 2 * HID), BF),
        pltpu.VMEM((R, 4 * HID), BF),
        pltpu.VMEM((NU, 2, N, BLK, U), BF),
        pltpu.VMEM((NU, N, BLK, U), BF),
        pltpu.VMEM((NU, N, BLK, U), BF),
        pltpu.VMEM((NU, N, BLK, U), BF),
        pltpu.VMEM((NU, T, C), BF),
        pltpu.VMEM((NU, T, C), BF),
        pltpu.VMEM((NU, 2, T, C), BF),
        pltpu.VMEM((4, H, HID), BF),
        pltpu.VMEM((2 * HID, H), BF),
        pltpu.SemaphoreType.DMA, sems(2), sems(3), sems(3), sems(3),
        sems(NP), sems(NP), sems(2, ND), sems(2, ND), sems(NP), sems(NP), sems(NP, 2), sems(NP, 2),
        sems(2, R // RB), sems(2, R // RB),
        sems(NU), sems(NU), sems(NU), sems(NU), sems(NU), sems(NU), sems(NU), sems(NU),
        sems(NU, 2), sems(NU, 2), sems(NU, 2),
        sems(NU, 3), sems(NU, 3), sems(NU, 3),
    ]
    shapes = [((T, D), BF), ((1, D, HID), BF), ((1, D, HID), BF), ((1, HID, D), BF)]
    held = pl.pallas_call(
        body,
        out_shape=[pltpu.VMEM(*shape) for shape in shapes],
        in_specs=[anyspace, anyspace, vmem, vmem, anyspace, anyspace, anyspace],
        out_specs=[anyspace] * 4,
        scratch_shapes=scratch,
        compiler_params=pltpu.CompilerParams(
            collective_id=0, has_side_effects=True, vmem_limit_bytes=47 * 1024 * 1024
        ),
        cost_estimate=pl.CostEstimate(flops=6_000_000_000, bytes_accessed=20_000_000, transcendentals=100_000),
    )(tokens, cotangent, expert_ids.T, gate_scores.T, gate_weight, up_weight, down_weight)
    held = [pltpu.with_memory_space_constraint(h, pltpu.VMEM) for h in held]
    return tuple(
        pl.pallas_call(
            write_out,
            out_shape=[jax.ShapeDtypeStruct(*shape) for shape in shapes],
            in_specs=[anyspace] * 4,
            out_specs=[anyspace] * 4,
            scratch_shapes=[sems(4)],
            compiler_params=pltpu.CompilerParams(vmem_limit_bytes=2 * 1024 * 1024),
        )(*held)
    )


def solution(mesh):
    placed = (
        P("ep", None),
        P("ep", None),
        P("ep", None),
        P("ep", None),
        P("ep", None, "grp"),
        P("ep", None, "grp"),
        P("ep", "grp", None),
    )
    return jax.shard_map(
        per_device,
        mesh=mesh,
        in_specs=placed,
        out_specs=(P("ep", None), P("ep", None, "grp"), P("ep", None, "grp"), P("ep", "grp", None)),
        check_vma=False,
    )
```

time: 119 us -> 99.4 us (0.84)
  local copies, waits for them, and re-layouts: 12.8 us -> 0 us
  Pallas kernels: 105 us -> 98.6 us
    unnamed x12 -> x0, local copies, waits for them, and re-layouts: 12.8 us -> none
    pallas_call x1 -> x2, Pallas kernels: 105 us -> 98.6 us  [the longest x1 94.9 us: per_device(): pl.pallas_call(body, out_shape=[pltpu.VMEM(*shape) for shape in shapes],...]
where the time goes in v2:
time: 99.4 us; the launch traced here: 99.2 us
  Pallas kernels  98.6 us (99%)
    pallas_call x1, Pallas kernels, per_device(): pl.pallas_call(body, out_shape=[pltpu.VMEM(*shape) for shape in shapes],...  94.9 us
    pallas_call x1, Pallas kernels, per_device(): pl.pallas_call(write_out, out_shape=[jax.ShapeDtypeStruct(*shape) for sha...  3.63 us

profile of v2, /device:TPU:1, one launch (start us, length us, event | category | flops | bytes accessed | tf_op | source)
XLA Modules:
  0.0 99.2 jit_solution(14441070847105664663)
XLA Ops:
  0.6 94.9 %shard_map.102 = (bf16[256,7168]{1,0:T(8,128)(2,1)S(1)}, bf16[1,7168,128]{2,1,0:T(8,128)(2,1)S(1)}, bf16[1,7168,128]{2,1,0:T(8,128)(2,1)S(1)}, bf16[1,128,7168]{2,1,0:T(8,128)(2,1)S(1)}) custom-call(bf16[256,7168]{1,0:T(8,128)(2,1)} %tok.1, bf16[256,7168]{1,0:T(8,128)(2,1)} %cot.1, s32[8,256]{1,0:T(8,128)} %bitcast.2, f32[8,256]{1,0:T(8,128)} %bitcast.3, ...), custom_call_target="tpu_custom_call" | custom-call | flops 6000000000 | bytes 20000000 | tf_op jit(solution)/shard_map/pallas_call | solution.py:516
  95.6 3.6 %shard_map.103 = (bf16[256,7168]{1,0:T(8,128)(2,1)}, bf16[1,7168,128]{2,1,0:T(8,128)(2,1)}, bf16[1,7168,128]{2,1,0:T(8,128)(2,1)}, bf16[1,128,7168]{2,1,0:T(8,128)(2,1)}) custom-call(bf16[256,7168]{1,0:T(8,128)(2,1)S(1)} %get-tuple-element.8.refs_0_, bf16[1,7168,128]{2,1,0:T(8,128)(2,1)S(1)} %get-tuple-element.9.refs_1_, ...), custom_call_target="tpu_custom_call" | custom-call | tf_op jit(solution)/shard_map/pallas_call | solution.py:529

commit v3 on v2

--- a/solution.py
+++ b/solution.py
@@ -23,7 +23,7 @@
 NU = H // W
 NA = H // C
 NP = 5
-ND = NA - 2 * NP
+ND = 6
 R16 = N * 16
 R8 = N * 8
 R = R16 + R8
@@ -63,16 +63,18 @@
     z, c = g // 2, g % 2
     x, y = e // SIDE, e % SIDE
     other = 1 - c
+    npc = NP - c
+    ndc = NA - 2 * npc
     za = z + 1 - 2 * (z % 2)
     zb = 3 - z
     zo = 3 - za
     sib = (2 * z + other, e)
 
     def first(i):
-        return za + (zb - za) * (i % 2)
+        return za + (zb - za) * ((i + c) % 2)
 
     def second(i):
-        return zb + (za - zb) * (i % 2)
+        return zb + (za - zb) * ((i + c) % 2)
 
     def at_z(zz):
         return (2 * zz + c, e)
@@ -98,11 +100,11 @@
         pl.semaphore_signal(bar, inc=1, device_id=dev, device_id_type=MESH)
 
     def load(src):
-        col = mult(c * H + (z % 2) * NP * C, C)
+        col = mult(c * H + (z % 2) * npc * C, C)
         return pltpu.make_async_copy(src.at[:, pl.ds(col, NP * C)], tokv, tok_sem)
 
     def load_d(a):
-        col = mult(c * H + 2 * NP * C, C)
+        col = mult(c * H + 2 * npc * C, C)
         return pltpu.make_async_copy((tok, cot)[a].at[:, pl.ds(col, ND * C)], tokd.at[a], tokd_sem.at[a])
 
     @pl.when(z < 2)
@@ -174,7 +176,7 @@
             remote(buf.at[dst], recv_a.at[n, e], ss, rs, (g, dst)).start()
 
     def part_of(owner, i):
-        return (owner // 2) * NA + (owner % 2) * NP + i
+        return (owner // 2) * NA + (owner % 2) * npc + i
 
     def dispatch(i, carry):
         src = tokv[:, pl.ds(mult(i * C, C), C)]
@@ -183,16 +185,17 @@
         spread(send_a.at[i], part_of(z, i), as_sem.at[i], ar_sem.at[i])
         return carry
 
-    def dispatch_d(d):
+    def dispatch_d(d, carry=0):
         for a in range(2):
             src = tokd[a, :, pl.ds(mult(d * C, C), C)]
             if a == 1:
                 src = (gate_col[...] * src.astype(F32)).astype(BF)
             pack(send_d.at[a, d], mm(pm[...], src))
-            spread(send_d.at[a, d], a * NA + 2 * NP + d, ds_a_sem.at[a, d], dr_a_sem.at[a, d])
+            spread(send_d.at[a, d], a * NA + 2 * npc + d, ds_a_sem.at[a, d], dr_a_sem.at[a, d])
+        return carry
 
     load(tok).wait()
-    lax.fori_loop(0, NP, dispatch, 0)
+    lax.fori_loop(0, npc, dispatch, 0)
     for a in range(2):
         load_d(a).wait()
 
@@ -209,7 +212,7 @@
         return remote(blocks, blocks, as_sem.at[i], ar_sem.at[i], sib)
 
     def arrived_d(a, d):
-        blocks = recv_a.at[a * NA + 2 * NP + d, pl.ds(0, N - 1)]
+        blocks = recv_a.at[a * NA + 2 * npc + d, pl.ds(0, N - 1)]
         return remote(blocks, blocks, ds_a_sem.at[a, d], dr_a_sem.at[a, d], sib)
 
     def unpack(a, m):
@@ -230,7 +233,7 @@
             acc_h[...] += mm(xm[1, :, cols], wd[:, cols], 1, 1)
 
     def process_of(owner, i):
-        a, m = owner // 2, (owner % 2) * NP + i
+        a, m = owner // 2, (owner % 2) * npc + i
         unpack(a, m)
 
         @pl.when(a == 0)
@@ -244,8 +247,8 @@
     def process_d(d):
         for a in range(2):
             arrived_d(a, d).wait_recv()
-            unpack(a, 2 * NP + d)
-            multiply(a, 2 * NP + d)
+            unpack(a, 2 * npc + d)
+            multiply(a, 2 * npc + d)
 
     def step1(i):
         blk = recv_a.at[part_of(z, i)]
@@ -262,15 +265,14 @@
         step1(i).start()
         step2(i, 0).start()
 
-        @pl.when(i + 1 < ND)
+        @pl.when(i + 1 < ndc)
         def _():
             dispatch_d(i + 1)
 
         return carry
 
-    lax.fori_loop(0, NP, gather1, 0)
-    for d in range(NP + 1, ND):
-        dispatch_d(d)
+    lax.fori_loop(0, npc, gather1, 0)
+    lax.fori_loop(npc + 1, ndc, dispatch_d, 0)
     for k in range(3):
         own_w[k].wait()
         sib_w[k].wait_recv()
@@ -281,18 +283,18 @@
         process_of(z, i)
         process_of(first(i), i)
 
-        @pl.when(i < ND)
+        @pl.when(i < ndc)
         def _():
             process_d(i)
 
         return carry
 
-    lax.fori_loop(0, NP, gather2, 0)
+    lax.fori_loop(0, npc, gather2, 0)
 
     def gather3(i, carry):
-        @pl.when(i + NP < ND)
-        def _():
-            process_d(i + NP)
+        @pl.when(i + npc < ndc)
+        def _():
+            process_d(i + npc)
 
         step2(i, 0).wait_recv()
         process_of(second(i), i)
@@ -300,7 +302,7 @@
         process_of(zo, i)
         return carry
 
-    lax.fori_loop(0, NP, gather3, 0)
+    lax.fori_loop(0, npc, gather3, 0)
 
     def swap(i):
         rows = pl.ds(mult(i * RB, RB), RB)
@@ -331,7 +333,7 @@
 
     def half(j):
         b = ((z + 1) // 2) % 2
-        return b + (z // 2 - b) * (j % 2)
+        return b + (z // 2 - b) * ((j + c) % 2)
 
     def pair(j):
         return remote(pk.at[j, 1 - half(j)], rsb.at[j], ps_sem.at[j], pr_sem.at[j], at_z(first(j)))
@@ -439,10 +441,14 @@
         step2(i, 1).wait_send()
         return carry
 
-    lax.fori_loop(0, NP, drain_a, 0)
-    for d in range(ND):
+    lax.fori_loop(0, npc, drain_a, 0)
+
+    def drain_d(d, carry):
         for a in range(2):
             arrived_d(a, d).wait_send()
+        return carry
+
+    lax.fori_loop(0, ndc, drain_d, 0)
 
     def drain(j, carry):
         blocks = send_c.at[j, pl.ds(0, N - 1)]

time: 99.4 us -> 97 us (0.976)
  Pallas kernels: 98.6 us -> 96.2 us
    pallas_call x1, Pallas kernels: 94.9 us -> 92.5 us  [per_device(): pl.pallas_call(body, out_shape=[pltpu.VMEM(*shape) for shape in shapes],...]
where the time goes in v3:
time: 97 us; the launch traced here: 96.8 us
  Pallas kernels  96.2 us (99%)
    pallas_call x1, Pallas kernels, per_device(): pl.pallas_call(body, out_shape=[pltpu.VMEM(*shape) for shape in shapes],...  92.5 us
    pallas_call x1, Pallas kernels, per_device(): pl.pallas_call(write_out, out_shape=[jax.ShapeDtypeStruct(*shape) for sha...  3.63 us

profile of v3, /device:TPU:1, one launch (start us, length us, event | category | flops | bytes accessed | tf_op | source)
XLA Modules:
  0.0 96.8 jit_solution(17793194458824947400)
XLA Ops:
  0.6 92.5 %shard_map.102 = (bf16[256,7168]{1,0:T(8,128)(2,1)S(1)}, bf16[1,7168,128]{2,1,0:T(8,128)(2,1)S(1)}, bf16[1,7168,128]{2,1,0:T(8,128)(2,1)S(1)}, bf16[1,128,7168]{2,1,0:T(8,128)(2,1)S(1)}) custom-call(bf16[256,7168]{1,0:T(8,128)(2,1)} %tok.1, bf16[256,7168]{1,0:T(8,128)(2,1)} %cot.1, s32[8,256]{1,0:T(8,128)} %bitcast.2, f32[8,256]{1,0:T(8,128)} %bitcast.3, ...), custom_call_target="tpu_custom_call" | custom-call | flops 6000000000 | bytes 20000000 | tf_op jit(solution)/shard_map/pallas_call | solution.py:522
  93.2 3.6 %shard_map.103 = (bf16[256,7168]{1,0:T(8,128)(2,1)}, bf16[1,7168,128]{2,1,0:T(8,128)(2,1)}, bf16[1,7168,128]{2,1,0:T(8,128)(2,1)}, bf16[1,128,7168]{2,1,0:T(8,128)(2,1)}) custom-call(bf16[256,7168]{1,0:T(8,128)(2,1)S(1)} %get-tuple-element.8.refs_0_, bf16[1,7168,128]{2,1,0:T(8,128)(2,1)S(1)} %get-tuple-element.9.refs_1_, ...), custom_call_target="tpu_custom_call" | custom-call | tf_op jit(solution)/shard_map/pallas_call | solution.py:535

commit v4 on v3

--- a/solution.py
+++ b/solution.py
@@ -33,7 +33,7 @@
     (1, 3), (3, 3), (1, 1), (3, 0), (0, 3), (1, 0), (0, 1),
 )
 RB = 128
-LAG = 2
+LAG = 4
 
 
 def mm(a, b, ca=1, cb=0):
@@ -166,9 +166,6 @@
         ),
     ]
 
-    for cp in sib_w:
-        cp.start()
-
     def spread(buf, n, ss, rs):
         recv_a[n, e] = buf[e]
         for k in range(N - 1):
@@ -196,6 +193,8 @@
 
     load(tok).wait()
     lax.fori_loop(0, npc, dispatch, 0)
+    for cp in sib_w:
+        cp.start()
     for a in range(2):
         load_d(a).wait()
 
@@ -283,18 +282,18 @@
         process_of(z, i)
         process_of(first(i), i)
 
-        @pl.when(i < ndc)
-        def _():
-            process_d(i)
+        @pl.when((i >= 1) & (i < ndc + 1))
+        def _():
+            process_d(i - 1)
 
         return carry
 
     lax.fori_loop(0, npc, gather2, 0)
 
     def gather3(i, carry):
-        @pl.when(i + npc < ndc)
-        def _():
-            process_d(i + npc)
+        @pl.when(i + npc - 1 < ndc)
+        def _():
+            process_d(i + npc - 1)
 
         step2(i, 0).wait_recv()
         process_of(second(i), i)

time: 97 us -> 94.9 us (0.978)
  Pallas kernels: 96.2 us -> 94.1 us
    pallas_call x1, Pallas kernels: 92.5 us -> 90.4 us  [per_device(): pl.pallas_call(body, out_shape=[pltpu.VMEM(*shape) for shape in shapes],...]
where the time goes in v4:
time: 94.9 us; the launch traced here: 94.7 us
  Pallas kernels  94.1 us (99%)
    pallas_call x1, Pallas kernels, per_device(): pl.pallas_call(body, out_shape=[pltpu.VMEM(*shape) for shape in shapes],...  90.4 us
    pallas_call x1, Pallas kernels, per_device(): pl.pallas_call(write_out, out_shape=[jax.ShapeDtypeStruct(*shape) for sha...  3.63 us

profile of v4, /device:TPU:1, one launch (start us, length us, event | category | flops | bytes accessed | tf_op | source)
XLA Modules:
  0.0 94.7 jit_solution(3960129166274166502)
XLA Ops:
  0.6 90.4 %shard_map.102 = (bf16[256,7168]{1,0:T(8,128)(2,1)S(1)}, bf16[1,7168,128]{2,1,0:T(8,128)(2,1)S(1)}, bf16[1,7168,128]{2,1,0:T(8,128)(2,1)S(1)}, bf16[1,128,7168]{2,1,0:T(8,128)(2,1)S(1)}) custom-call(bf16[256,7168]{1,0:T(8,128)(2,1)} %tok.1, bf16[256,7168]{1,0:T(8,128)(2,1)} %cot.1, s32[8,256]{1,0:T(8,128)} %bitcast.2, f32[8,256]{1,0:T(8,128)} %bitcast.3, ...), custom_call_target="tpu_custom_call" | custom-call | flops 6000000000 | bytes 20000000 | tf_op jit(solution)/shard_map/pallas_call | solution.py:521
  91.1 3.6 %shard_map.103 = (bf16[256,7168]{1,0:T(8,128)(2,1)}, bf16[1,7168,128]{2,1,0:T(8,128)(2,1)}, bf16[1,7168,128]{2,1,0:T(8,128)(2,1)}, bf16[1,128,7168]{2,1,0:T(8,128)(2,1)}) custom-call(bf16[256,7168]{1,0:T(8,128)(2,1)S(1)} %get-tuple-element.8.refs_0_, bf16[1,7168,128]{2,1,0:T(8,128)(2,1)S(1)} %get-tuple-element.9.refs_1_, ...), custom_call_target="tpu_custom_call" | custom-call | tf_op jit(solution)/shard_map/pallas_call | solution.py:534

commit v5 on v4

--- a/solution.py
+++ b/solution.py
@@ -34,6 +34,8 @@
 )
 RB = 128
 LAG = 4
+GL = 3
+N1 = 2
 
 
 def mm(a, b, ca=1, cb=0):
@@ -53,9 +55,10 @@
     o_tok, o_gate, o_up, o_down,
     tokv, tokd, pm, q16, q8a, q8b, scale, gate_col,
     send_a, send_d, recv_a, xm, wgu, wd, acc_gu, acc_h, accr_gu, accr_h, hid, g2,
-    pk, rsb, send_c, recv_c, zp, zr, fin, dwgu, dwd,
+    pk, rsb, send_c, recv_c, recv_i, zx, zy, zp, zr, fin, dwgu, dwd,
     tok_sem, tokd_sem, w_sem, ws_sem, wr_sem, as_sem, ar_sem, ds_a_sem, dr_a_sem, z1s_sem, z1r_sem, z2s_sem, z2r_sem,
     bs_sem, br_sem, ps_sem, pr_sem, cs_sem, cr_sem, xs_sem, xr_sem, gs_sem, gr_sem,
+    is_sem, ir_sem, ts_sem, tr_sem,
     ol_sem, os_sem, or_sem, dl_sem, ds_sem, dr_sem,
 ):
     g = lax.axis_index("grp")
@@ -337,16 +340,32 @@
     def pair(j):
         return remote(pk.at[j, 1 - half(j)], rsb.at[j], ps_sem.at[j], pr_sem.at[j], at_z(first(j)))
 
-    def row_grad(j, carry):
+    def row_grad(j):
         cols = pl.ds(mult(j * W, W), W)
         w = jnp.concatenate([wgu[i, cols, :] for i in range(4)], axis=1)
         r = mm(g2[...], w, 1, 1)
         for h in range(2):
             pack(pk.at[j, h], r[:, h * C : (h + 1) * C])
+
+    def early(j, carry):
+        row_grad(j)
+        for h in range(2):
+            recv_i[j, h, e] = pk[j, h, e]
+            for k in range(N - 1):
+                dst = peer(k)
+                remote(
+                    pk.at[j, h, dst], recv_i.at[j, h, e], is_sem.at[j, h], ir_sem.at[j, h], (g, dst)
+                ).start()
+        return carry
+
+    def summed(j, carry):
+        row_grad(j)
         pair(j).start()
         return carry
 
-    lax.fori_loop(0, NU, row_grad, 0)
+    lax.fori_loop(0, 1, early, 0)
+    lax.fori_loop(N1, NU, summed, 0)
+    lax.fori_loop(1, N1, early, 0)
 
     def back(j, carry):
         pair(j).wait_recv()
@@ -357,7 +376,14 @@
             remote(send_c.at[j, dst], recv_c.at[j, e], cs_sem.at[j], cr_sem.at[j], (g, dst)).start()
         return carry
 
-    lax.fori_loop(0, NU, back, 0)
+    lax.fori_loop(N1, NU, back, 0)
+
+    def early_all(j, h):
+        blocks = recv_i.at[j, h, pl.ds(0, N - 1)]
+        return remote(blocks, blocks, is_sem.at[j, h], ir_sem.at[j, h], sib)
+
+    def give(j):
+        return remote(zx.at[j], zy.at[j], ts_sem.at[j], tr_sem.at[j], at_z(first(j)))
 
     def cross(j):
         return remote(zp.at[j], zr.at[j], xs_sem.at[j], xr_sem.at[j], at_z(second(j)))
@@ -387,31 +413,63 @@
         far.append(remote(dwd.at[yours, rows], o_down.at[0, :, orow], ds_sem.at[j, 2], dr_sem.at[j, 2], sib))
         return local, far
 
+    def scatter(r):
+        r8 = r[:, 32:48, :].reshape(R16, U)
+        parts = []
+        for p in range(2):
+            r16 = r[:, 16 * p : 16 * p + 16, :].reshape(R16, U)
+            parts.append((mm(q16[...], r16) + mm((q8a, q8b)[p][...], r8)).astype(BF))
+        return jnp.concatenate(parts, axis=1)
+
+    def crossed(j):
+        cross(j).wait_recv()
+        fin[j, half(j)] = (zp[j].astype(F32) + zr[j].astype(F32)).astype(BF)
+        whole(j).start()
+
+    def finished(j):
+        whole(j).wait_recv()
+        for p in range(2):
+            out_local(j, p).start()
+            out_sib(j, p).start()
+
     def pipe(t, carry):
-        @pl.when(t < NU)
+        @pl.when(t < N1)
+        def _():
+            for h in range(2):
+                early_all(t, h).wait_recv()
+            zx[t] = scatter(recv_i[t, 1 - half(t)])
+            give(t).start()
+            zp[t] = scatter(recv_i[t, half(t)])
+
+        @pl.when((t >= N1) & (t < NU))
         def _():
             blocks = recv_c.at[t, pl.ds(0, N - 1)]
             remote(blocks, blocks, cs_sem.at[t], cr_sem.at[t], sib).wait_recv()
-            r = recv_c[t]
-            r8 = r[:, 32:48, :].reshape(R16, U)
-            for p in range(2):
-                r16 = r[:, 16 * p : 16 * p + 16, :].reshape(R16, U)
-                zp[t, :, p * U : (p + 1) * U] = (mm(q16[...], r16) + mm((q8a, q8b)[p][...], r8)).astype(BF)
+            zp[t] = scatter(recv_c[t])
             cross(t).start()
 
-        @pl.when((t >= LAG) & (t < NU + LAG))
-        def _():
-            j = t - LAG
-            cross(j).wait_recv()
-            fin[j, half(j)] = (zp[j].astype(F32) + zr[j].astype(F32)).astype(BF)
-            whole(j).start()
-
-        @pl.when(t >= 2 * LAG)
-        def _():
-            whole(t - 2 * LAG).wait_recv()
-            for p in range(2):
-                out_local(t - 2 * LAG, p).start()
-                out_sib(t - 2 * LAG, p).start()
+        @pl.when((t >= GL) & (t < N1 + GL))
+        def _():
+            j = t - GL
+            give(j).wait_recv()
+            zp[j] = (zp[j].astype(F32) + zy[j].astype(F32)).astype(BF)
+            cross(j).start()
+
+        @pl.when((t >= GL + LAG) & (t < N1 + GL + LAG))
+        def _():
+            crossed(t - GL - LAG)
+
+        @pl.when((t >= N1 + LAG) & (t < NU + LAG))
+        def _():
+            crossed(t - LAG)
+
+        @pl.when((t >= GL + 2 * LAG) & (t < N1 + GL + 2 * LAG))
+        def _():
+            finished(t - GL - 2 * LAG)
+
+        @pl.when(t >= N1 + 2 * LAG)
+        def _():
+            finished(t - 2 * LAG)
 
         @pl.when(t < NU)
         def _():
@@ -449,10 +507,21 @@
 
     lax.fori_loop(0, ndc, drain_d, 0)
 
-    def drain(j, carry):
+    for j in range(N1):
+        give(j).wait_send()
+        for h in range(2):
+            early_all(j, h).wait_send()
+
+    def drain_c(j, carry):
         blocks = send_c.at[j, pl.ds(0, N - 1)]
         remote(blocks, blocks, cs_sem.at[j], cr_sem.at[j], sib).wait_send()
-        for cp in (pair(j), cross(j), whole(j)):
+        pair(j).wait_send()
+        return carry
+
+    lax.fori_loop(N1, NU, drain_c, 0)
+
+    def drain(j, carry):
+        for cp in (cross(j), whole(j)):
             cp.wait_send()
         for p in range(2):
             out_local(j, p).wait()
@@ -505,6 +574,9 @@
         pltpu.VMEM((NU, N, BLK, U), BF),
         pltpu.VMEM((NU, N, BLK, U), BF),
         pltpu.VMEM((NU, N, BLK, U), BF),
+        pltpu.VMEM((N1, 2, N, BLK, U), BF),
+        pltpu.VMEM((N1, T, C), BF),
+        pltpu.VMEM((N1, T, C), BF),
         pltpu.VMEM((NU, T, C), BF),
         pltpu.VMEM((NU, T, C), BF),
         pltpu.VMEM((NU, 2, T, C), BF),
@@ -514,6 +586,7 @@
         sems(NP), sems(NP), sems(2, ND), sems(2, ND), sems(NP), sems(NP), sems(NP, 2), sems(NP, 2),
         sems(2, R // RB), sems(2, R // RB),
         sems(NU), sems(NU), sems(NU), sems(NU), sems(NU), sems(NU), sems(NU), sems(NU),
+        sems(N1, 2), sems(N1, 2), sems(N1), sems(N1),
         sems(NU, 2), sems(NU, 2), sems(NU, 2),
         sems(NU, 3), sems(NU, 3), sems(NU, 3),
     ]

time: 94.9 us -> 94.6 us (level)
  no operation moved by 1% of the time
where the time goes in v5:
time: 94.6 us; the launch traced here: 94.4 us
  Pallas kernels  93.7 us (99%)
    pallas_call x1, Pallas kernels, per_device(): pl.pallas_call(body, out_shape=[pltpu.VMEM(*shape) for shape in shapes],...  90.1 us
    pallas_call x1, Pallas kernels, per_device(): pl.pallas_call(write_out, out_shape=[jax.ShapeDtypeStruct(*shape) for sha...  3.63 us

profile of v5, /device:TPU:1, one launch (start us, length us, event | category | flops | bytes accessed | tf_op | source)
XLA Modules:
  0.0 94.4 jit_solution(8034826379383489826)
XLA Ops:
  0.6 90.1 %shard_map.102 = (bf16[256,7168]{1,0:T(8,128)(2,1)S(1)}, bf16[1,7168,128]{2,1,0:T(8,128)(2,1)S(1)}, bf16[1,7168,128]{2,1,0:T(8,128)(2,1)S(1)}, bf16[1,128,7168]{2,1,0:T(8,128)(2,1)S(1)}) custom-call(bf16[256,7168]{1,0:T(8,128)(2,1)} %tok.1, bf16[256,7168]{1,0:T(8,128)(2,1)} %cot.1, s32[8,256]{1,0:T(8,128)} %bitcast.2, f32[8,256]{1,0:T(8,128)} %bitcast.3, ...), custom_call_target="tpu_custom_call" | custom-call | flops 6000000000 | bytes 20000000 | tf_op jit(solution)/shard_map/pallas_call | solution.py:594
  90.7 3.6 %shard_map.103 = (bf16[256,7168]{1,0:T(8,128)(2,1)}, bf16[1,7168,128]{2,1,0:T(8,128)(2,1)}, bf16[1,7168,128]{2,1,0:T(8,128)(2,1)}, bf16[1,128,7168]{2,1,0:T(8,128)(2,1)}) custom-call(bf16[256,7168]{1,0:T(8,128)(2,1)S(1)} %get-tuple-element.8.refs_0_, bf16[1,7168,128]{2,1,0:T(8,128)(2,1)S(1)} %get-tuple-element.9.refs_1_, ...), custom_call_target="tpu_custom_call" | custom-call | tf_op jit(solution)/shard_map/pallas_call | solution.py:607

commit v6 on v5

--- a/solution.py
+++ b/solution.py
@@ -35,7 +35,7 @@
 RB = 128
 LAG = 4
 GL = 3
-N1 = 2
+N1 = 3
 
 
 def mm(a, b, ca=1, cb=0):

time: 94.6 us -> 97.3 us (1.029)
  Pallas kernels: 93.7 us -> 96.5 us
    pallas_call x1, Pallas kernels: 90.1 us -> 92.8 us  [per_device(): pl.pallas_call(body, out_shape=[pltpu.VMEM(*shape) for shape in shapes],...]
where the time goes in v6:
time: 97.3 us; the launch traced here: 97.1 us
  Pallas kernels  96.5 us (99%)
    pallas_call x1, Pallas kernels, per_device(): pl.pallas_call(body, out_shape=[pltpu.VMEM(*shape) for shape in shapes],...  92.8 us
    pallas_call x1, Pallas kernels, per_device(): pl.pallas_call(write_out, out_shape=[jax.ShapeDtypeStruct(*shape) for sha...  3.63 us

profile of v6, /device:TPU:1, one launch (start us, length us, event | category | flops | bytes accessed | tf_op | source)
XLA Modules:
  0.0 97.1 jit_solution(6009630836966141670)
XLA Ops:
  0.6 92.8 %shard_map.102 = (bf16[256,7168]{1,0:T(8,128)(2,1)S(1)}, bf16[1,7168,128]{2,1,0:T(8,128)(2,1)S(1)}, bf16[1,7168,128]{2,1,0:T(8,128)(2,1)S(1)}, bf16[1,128,7168]{2,1,0:T(8,128)(2,1)S(1)}) custom-call(bf16[256,7168]{1,0:T(8,128)(2,1)} %tok.1, bf16[256,7168]{1,0:T(8,128)(2,1)} %cot.1, s32[8,256]{1,0:T(8,128)} %bitcast.2, f32[8,256]{1,0:T(8,128)} %bitcast.3, ...), custom_call_target="tpu_custom_call" | custom-call | flops 6000000000 | bytes 20000000 | tf_op jit(solution)/shard_map/pallas_call | solution.py:594
  93.5 3.6 %shard_map.103 = (bf16[256,7168]{1,0:T(8,128)(2,1)}, bf16[1,7168,128]{2,1,0:T(8,128)(2,1)}, bf16[1,7168,128]{2,1,0:T(8,128)(2,1)}, bf16[1,128,7168]{2,1,0:T(8,128)(2,1)}) custom-call(bf16[256,7168]{1,0:T(8,128)(2,1)S(1)} %get-tuple-element.8.refs_0_, bf16[1,7168,128]{2,1,0:T(8,128)(2,1)S(1)} %get-tuple-element.9.refs_1_, ...), custom_call_target="tpu_custom_call" | custom-call | tf_op jit(solution)/shard_map/pallas_call | solution.py:607
